TPU v7x, 1024 devices: a whole 4x4x32 slice. The times are simulated.
1024 devices in a mesh: ctx: 128 (over x, z), head: 8 (over y, core).
Axes of the slice: x: 4, y: 4, z: 32, core: 2. Of those that a mesh axis runs over, the one named last changes fastest.
Arguments:
- queries: bfloat16 [16384, 12288], P('ctx', 'head'), may hold values from -6 to 6, as said below
- keys: bfloat16 [16384, 1024], P('ctx', 'head'), may hold values from -6 to 6
- values: bfloat16 [16384, 1024], P('ctx', 'head'), may hold values from -6 to 6
- out_grad: bfloat16 [16384, 12288], P('ctx', 'head'), may hold values from -45 to 45
- doc_lengths: int32 [32], replicated, may hold values from 1 to 1024, 16384 in all
Outputs:
- grad_queries: bfloat16 [16384, 12288], P('ctx', 'head')
- grad_keys: bfloat16 [16384, 1024], P('ctx', 'head')
- grad_values: bfloat16 [16384, 1024], P('ctx', 'head')
- grad_rms: float32 [], replicated
Inputs may be any that keep to these rules, and one draw needn't show every extreme that they name: `queries`: query and key entries lie within the stated range. `doc_lengths`: the lengths sum to 16384; the longest is exactly 1024.
All inputs are finite; a program needn't handle non-finite values.
Results may differ from a plain program's by a relative error of at most 0.0084.
Values may be sent and summed in bfloat16 or wider, within the bound.
A program may use at most 32 MiB of HBM per device.

v0:
```python
from functools import partial
import math

import jax
import jax.numpy as jnp
from jax import lax
from jax.sharding import PartitionSpec as P

QH = 96
KVH = 8
HD = 128


def passed_along(value, axis, steps):
    count = lax.axis_size(axis)
    leading, last = (max(0, -steps), min(count, count - steps))
    return lax.ppermute(value, axis, [(source, source + steps) for source in range(leading, last)])


def token_starts(doc_lengths, positions):
    starts = jnp.cumsum(doc_lengths, dtype=jnp.int32) - doc_lengths
    before = starts[None, :] <= positions[:, None]
    return jnp.max(jnp.where(before, starts[None, :], 0), axis=1)


def head_group(carry, inputs, keys_one, values_one, allowed, score_scale):
    dk_total, dv_total = carry
    query_part, grad_part = inputs
    scores = (
        jnp.einsum("qgd,kd->gqk", query_part, keys_one, preferred_element_type=jnp.float32)
        * score_scale
    )
    scores = jnp.where(allowed[None], scores, -jnp.inf)
    peak = jnp.max(scores, axis=2, keepdims=True)
    log_total = peak + jnp.log(jnp.sum(jnp.exp(scores - peak), axis=2, keepdims=True))
    weights = jnp.where(allowed[None], jnp.exp(scores - log_total), 0.0)
    weights_low = weights.astype(jnp.bfloat16)
    attended = jnp.einsum(
        "gqk,kd->qgd", weights_low, values_one, preferred_element_type=jnp.float32
    )
    row_dots = jnp.sum(grad_part.astype(jnp.float32) * attended, axis=2)
    grad_weights = jnp.einsum(
        "qgd,kd->gqk", grad_part, values_one, preferred_element_type=jnp.float32
    )
    grad_scores = (weights * (grad_weights - row_dots.T[:, :, None])).astype(jnp.bfloat16)
    grad_query = (
        jnp.einsum("gqk,kd->qgd", grad_scores, keys_one, preferred_element_type=jnp.float32)
        * score_scale
    )
    dk_total = (
        dk_total
        + jnp.einsum("gqk,qgd->kd", grad_scores, query_part, preferred_element_type=jnp.float32)
        * score_scale
    )
    dv_total = dv_total + jnp.einsum(
        "gqk,qgd->kd", weights_low, grad_part, preferred_element_type=jnp.float32
    )
    return ((dk_total, dv_total), grad_query)


def local(queries, keys, values, out_grad, doc_lengths):
    tok_rows = queries.shape[0]
    kv_local = keys.shape[1] // HD
    group_size = QH // KVH
    ctx_count = lax.axis_size("ctx")
    reach_tiles = min(8, ctx_count // 2)
    ctx_index = lax.axis_index("ctx")
    window = (reach_tiles + 1) * tok_rows
    query_pos = ctx_index * tok_rows + jnp.arange(tok_rows, dtype=jnp.int32)
    key_pos = (ctx_index - reach_tiles) * tok_rows + jnp.arange(window, dtype=jnp.int32)
    first_allowed = token_starts(doc_lengths, query_pos)
    allowed = (key_pos[None, :] >= first_allowed[:, None]) & (
        key_pos[None, :] <= query_pos[:, None]
    )
    paired = jnp.stack([keys, values])
    arrived = [paired]
    current = paired
    for hop_count in range(reach_tiles):
        current = passed_along(current, "ctx", 1)
        arrived.append(current)
    gathered = jnp.concatenate(arrived[::-1], axis=1)
    score_scale = HD ** (-0.5)
    split_size = math.gcd(group_size, 4)
    rounds = group_size // split_size
    query_heads = queries.reshape(tok_rows, kv_local, rounds, split_size, HD)
    grad_heads = out_grad.reshape(tok_rows, kv_local, rounds, split_size, HD)
    keys_one = gathered[0, :, 0:HD]
    values_one = gathered[1, :, 0:HD]
    inputs = (jnp.moveaxis(query_heads[:, 0], 1, 0), jnp.moveaxis(grad_heads[:, 0], 1, 0))
    zeros = jnp.zeros((window, HD), jnp.float32)
    stepper = partial(
        head_group,
        keys_one=keys_one,
        values_one=values_one,
        allowed=allowed,
        score_scale=score_scale,
    )
    (dk_total, dv_total), grad_query = lax.scan(stepper, (zeros, zeros), inputs)
    dq_parts = jnp.moveaxis(grad_query, 0, 1).reshape(tok_rows, group_size * HD)
    partial_kv = jnp.stack([dk_total, dv_total])

    def source_piece(distance):
        offset = (reach_tiles - distance) * tok_rows
        return partial_kv[:, offset : offset + tok_rows]

    carried = jnp.zeros((2, tok_rows, partial_kv.shape[2]), jnp.float32)
    for distance in range(reach_tiles, 0, -1):
        carried = passed_along(carried + source_piece(distance), "ctx", -1)
    owned = carried + source_piece(0)
    local_squares = jnp.sum(dq_parts * dq_parts) + jnp.sum(owned * owned)
    total = lax.psum(local_squares, ("ctx", "head"))
    count_all = ctx_count * tok_rows * (QH * HD + 2 * KVH * HD)
    grad_rms = jnp.sqrt(total / count_all)
    return (
        dq_parts.astype(jnp.bfloat16),
        owned[0].astype(jnp.bfloat16),
        owned[1].astype(jnp.bfloat16),
        grad_rms,
    )


def solution(mesh):
    return jax.shard_map(
        local,
        mesh=mesh,
        in_specs=(P("ctx", "head"), P("ctx", "head"), P("ctx", "head"), P("ctx", "head"), P()),
        out_specs=(P("ctx", "head"), P("ctx", "head"), P("ctx", "head"), P()),
        check_vma=False,
    )
```

profile of v0, /device:TPU:1, one launch (start us, length us, event | category | flops | bytes accessed | tf_op | source)
XLA Modules:
  0.0 353.1 jit_solution(8567557054585938554)
XLA Ops:
  1.5 4.4 %collective-permute-start = (bf16[2,128,128]{2,1,0:T(8,128)(2,1)S(1)}, bf16[2,128,128]{2,1,0:T(8,128)(2,1)S(1)}, u32[]{:S(2)}, u32[]{:S(2)}) collective-permute-start(bf16[2,128,128]{2,1,0:T(8,128)(2,1)S(1)} %pad_maximum_fusion.1), channel_id=1, source_target_pairs={{0,8},{8,16},{16,24},{24,32},{32,40},{40,48},{48,56},{56,64},{64,7... | collective-permute-start | bytes 196616 | tf_op jit(solution)/shard_map/ppermute | solution.py:17
  5.9 1.3 collective-permute-done
  7.2 3.8 %collective-permute-start.1 = (bf16[2,128,128]{2,1,0:T(8,128)(2,1)S(1)}, bf16[2,128,128]{2,1,0:T(8,128)(2,1)S(1)}, u32[]{:S(2)}, u32[]{:S(2)}) collective-permute-start(bf16[2,128,128]{2,1,0:T(8,128)(2,1)S(1)} %collective-permute-done), channel_id=1, source_target_pairs={{0,8},{8,16},{16,24},{24,32},{32,40},{40,48},{48,56},{56,64},{64,7... | collective-permute-start | bytes 196616 | tf_op jit(solution)/shard_map/ppermute | solution.py:17
  11.0 1.3 collective-permute-done.1
  12.3 3.7 %collective-permute-start.2 = (bf16[2,128,128]{2,1,0:T(8,128)(2,1)S(1)}, bf16[2,128,128]{2,1,0:T(8,128)(2,1)S(1)}, u32[]{:S(2)}, u32[]{:S(2)}) collective-permute-start(bf16[2,128,128]{2,1,0:T(8,128)(2,1)S(1)} %collective-permute-done.1), channel_id=1, source_target_pairs={{0,8},{8,16},{16,24},{24,32},{32,40},{40,48},{48,56},{56,64},{64,7... | collective-permute-start | bytes 196616 | tf_op jit(solution)/shard_map/ppermute | solution.py:17
  16.0 1.3 collective-permute-done.2
  17.3 4.3 %collective-permute-start.3 = (bf16[2,128,128]{2,1,0:T(8,128)(2,1)S(1)}, bf16[2,128,128]{2,1,0:T(8,128)(2,1)S(1)}, u32[]{:S(2)}, u32[]{:S(2)}) collective-permute-start(bf16[2,128,128]{2,1,0:T(8,128)(2,1)S(1)} %collective-permute-done.2), channel_id=1, source_target_pairs={{0,8},{8,16},{16,24},{24,32},{32,40},{40,48},{48,56},{56,64},{64,7... | collective-permute-start | bytes 196616 | tf_op jit(solution)/shard_map/ppermute | solution.py:17
  21.6 1.3 collective-permute-done.3
  22.9 4.9 %collective-permute-start.4 = (bf16[2,128,128]{2,1,0:T(8,128)(2,1)S(1)}, bf16[2,128,128]{2,1,0:T(8,128)(2,1)S(1)}, u32[]{:S(2)}, u32[]{:S(2)}) collective-permute-start(bf16[2,128,128]{2,1,0:T(8,128)(2,1)S(1)} %collective-permute-done.3), channel_id=1, source_target_pairs={{0,8},{8,16},{16,24},{24,32},{32,40},{40,48},{48,56},{56,64},{64,7... | collective-permute-start | bytes 196616 | tf_op jit(solution)/shard_map/ppermute | solution.py:17
  29.4 1.9 copy.32
  31.4 1.9 copy.33
  33.3 4.9 %collective-permute-start.5 = (bf16[2,128,128]{2,1,0:T(8,128)(2,1)S(1)}, bf16[2,128,128]{2,1,0:T(8,128)(2,1)S(1)}, u32[]{:S(2)}, u32[]{:S(2)}) collective-permute-start(bf16[2,128,128]{2,1,0:T(8,128)(2,1)S(1)} %collective-permute-done.4), channel_id=1, source_target_pairs={{0,8},{8,16},{16,24},{24,32},{32,40},{40,48},{48,56},{56,64},{64,7... | collective-permute-start | bytes 196616 | tf_op jit(solution)/shard_map/ppermute | solution.py:17
  38.2 1.3 collective-permute-done.5
  39.5 5.2 %collective-permute-start.6 = (bf16[2,128,128]{2,1,0:T(8,128)(2,1)S(1)}, bf16[2,128,128]{2,1,0:T(8,128)(2,1)S(1)}, u32[]{:S(2)}, u32[]{:S(2)}) collective-permute-start(bf16[2,128,128]{2,1,0:T(8,128)(2,1)S(1)} %collective-permute-done.5), channel_id=1, source_target_pairs={{0,8},{8,16},{16,24},{24,32},{32,40},{40,48},{48,56},{56,64},{64,7... | collective-permute-start | bytes 196616 | tf_op jit(solution)/shard_map/ppermute | solution.py:17
  46.0 4.6 %collective-permute-start.7 = (bf16[2,128,128]{2,1,0:T(8,128)(2,1)S(1)}, bf16[2,128,128]{2,1,0:T(8,128)(2,1)S(1)}, u32[]{:S(2)}, u32[]{:S(2)}) collective-permute-start(bf16[2,128,128]{2,1,0:T(8,128)(2,1)S(1)} %collective-permute-done.6), channel_id=1, source_target_pairs={{0,8},{8,16},{16,24},{24,32},{32,40},{40,48},{48,56},{56,64},{64,7... | collective-permute-start | bytes 196616 | tf_op jit(solution)/shard_map/ppermute | solution.py:17
  50.6 1.3 collective-permute-done.7
  53.8 41.2 %while.15 = (s32[]{:T(128)}, f32[1152,128]{1,0:T(8,128)S(1)}, f32[1152,128]{1,0:T(8,128)S(1)}, f32[3,128,4,128]{3,1,2,0:T(8,128)}, bf16[3,128,4,128]{1,3,2,0:T(8...) while((s32[]{:T(128)}, f32[1152,128]{1,0:T(8,128)S(1)}, ...), condition=%wide.region_6.7_spmd.clone, body=%wide.region_2.6_spmd.clone.sunk | while | flops 916847616 | bytes 25150800 | solution.py:98
  54.6 1.7 fusion.77
  56.8 1.6 constant_dynamic-slice_fusion.2
  58.4 1.8 fusion.81
  60.2 1.7 copy.47
  61.9 1.8 fusion.78
  65.8 1.7 fusion.80
  68.4 1.7 fusion.77
  70.6 1.6 constant_dynamic-slice_fusion.2
  72.2 1.8 fusion.81
  73.9 1.7 copy.47
  75.6 1.8 fusion.78
  79.5 1.7 fusion.80
  82.1 1.7 fusion.77
  84.3 1.6 constant_dynamic-slice_fusion.2
  85.9 1.8 fusion.81
  87.7 1.7 copy.47
  89.4 1.8 fusion.78
  93.3 1.7 fusion.80
  95.0 1.3 collective-permute-start.8
  96.3 4.7 %collective-permute-done.8 = f32[2,128,128]{2,1,0:T(8,128)S(1)} collective-permute-done((f32[2,128,128]{2,1,0:T(8,128)S(1)}, f32[2,128,128]{2,1,0:T(8,128)S(1)}, u32[]{:S(2)}, u32[]{:S(2)}) %collective-permute-start.8) | collective-permute-done | bytes 131104 | tf_op jit(solution)/shard_map/ppermute | solution.py:17
  101.1 1.3 collective-permute-start.9
  102.4 4.7 %collective-permute-done.9 = f32[2,128,128]{2,1,0:T(8,128)S(1)} collective-permute-done((f32[2,128,128]{2,1,0:T(8,128)S(1)}, f32[2,128,128]{2,1,0:T(8,128)S(1)}, u32[]{:S(2)}, u32[]{:S(2)}) %collective-permute-start.9) | collective-permute-done | bytes 131104 | tf_op jit(solution)/shard_map/ppermute | solution.py:17
  107.1 1.3 collective-permute-start.10
  108.4 5.7 %collective-permute-done.10 = f32[2,128,128]{2,1,0:T(8,128)S(1)} collective-permute-done((f32[2,128,128]{2,1,0:T(8,128)S(1)}, f32[2,128,128]{2,1,0:T(8,128)S(1)}, u32[]{:S(2)}, u32[]{:S(2)}) %collective-permute-start.10) | collective-permute-done | bytes 131104 | tf_op jit(solution)/shard_map/ppermute | solution.py:17
  115.4 5.9 %collective-permute-done.11 = f32[2,128,128]{2,1,0:T(8,128)S(1)} collective-permute-done((f32[2,128,128]{2,1,0:T(8,128)S(1)}, f32[2,128,128]{2,1,0:T(8,128)S(1)}, u32[]{:S(2)}, u32[]{:S(2)}) %collective-permute-start.11) | collective-permute-done | bytes 131104 | tf_op jit(solution)/shard_map/ppermute | solution.py:17
  121.3 1.4 collective-permute-start.12
  122.8 5.6 %collective-permute-done.12 = f32[2,128,128]{2,1,0:T(8,128)S(1)} collective-permute-done((f32[2,128,128]{2,1,0:T(8,128)S(1)}, f32[2,128,128]{2,1,0:T(8,128)S(1)}, u32[]{:S(2)}, u32[]{:S(2)}) %collective-permute-start.12) | collective-permute-done | bytes 131104 | tf_op jit(solution)/shard_map/ppermute | solution.py:17
  129.7 5.6 %collective-permute-done.13 = f32[2,128,128]{2,1,0:T(8,128)S(1)} collective-permute-done((f32[2,128,128]{2,1,0:T(8,128)S(1)}, f32[2,128,128]{2,1,0:T(8,128)S(1)}, u32[]{:S(2)}, u32[]{:S(2)}) %collective-permute-start.13) | collective-permute-done | bytes 131104 | tf_op jit(solution)/shard_map/ppermute | solution.py:17
  136.7 5.9 %collective-permute-done.14 = f32[2,128,128]{2,1,0:T(8,128)S(1)} collective-permute-done((f32[2,128,128]{2,1,0:T(8,128)S(1)}, f32[2,128,128]{2,1,0:T(8,128)S(1)}, u32[]{:S(2)}, u32[]{:S(2)}) %collective-permute-start.14) | collective-permute-done | bytes 131104 | tf_op jit(solution)/shard_map/ppermute | solution.py:17
  145.0 6.4 %collective-permute-done.15 = f32[2,128,128]{2,1,0:T(8,128)S(1)} collective-permute-done((f32[2,128,128]{2,1,0:T(8,128)S(1)}, f32[2,128,128]{2,1,0:T(8,128)S(1)}, u32[]{:S(2)}, u32[]{:S(2)}) %collective-permute-start.15) | collective-permute-done | bytes 131104 | tf_op jit(solution)/shard_map/ppermute | solution.py:17
  154.3 196.3 %psum.7 = f32[]{:T(128)} all-reduce(f32[]{:T(128)S(6)} %add.79), channel_id=1, replica_groups=mesh['ctx'=128,'head'=8] {'ctx','head'}, use_global_device_ids=true, to_apply=%region_9.10 | all-reduce | flops 1 | bytes 8 | tf_op jit(solution)/shard_map/psum | solution.py:111
  (104 shorter events, 24.5 us)
Async XLA Ops:
  0.6 51.4 %copy-start.7 = (bf16[128,128]{1,0:T(8,128)(2,1)S(1)}, bf16[128,128]{1,0:T(8,128)(2,1)}, u32[]{:S(2)}) copy-start(bf16[128,128]{1,0:T(8,128)(2,1)} %param.8) | copy-start | bytes 98308
  0.6 51.4 %copy-start.6 = (bf16[128,128]{1,0:T(8,128)(2,1)S(1)}, bf16[128,128]{1,0:T(8,128)(2,1)}, u32[]{:S(2)}) copy-start(bf16[128,128]{1,0:T(8,128)(2,1)} %param.9) | copy-start | bytes 98308
  1.5 5.7 %collective-permute-start = (bf16[2,128,128]{2,1,0:T(8,128)(2,1)S(1)}, bf16[2,128,128]{2,1,0:T(8,128)(2,1)S(1)}, u32[]{:S(2)}, u32[]{:S(2)}) collective-permute-start(bf16[2,128,128]{2,1,0:T(8,128)(2,1)S(1)} %pad_maximum_fusion.1), channel_id=1, source_target_pairs={{0,8},{8,16},{16,24},{24,32},{32,40},{40,48},{48,56},{56,64},{64,7... | collective-permute-start | bytes 196616 | tf_op jit(solution)/shard_map/ppermute | solution.py:17
  7.2 5.1 %collective-permute-start.1 = (bf16[2,128,128]{2,1,0:T(8,128)(2,1)S(1)}, bf16[2,128,128]{2,1,0:T(8,128)(2,1)S(1)}, u32[]{:S(2)}, u32[]{:S(2)}) collective-permute-start(bf16[2,128,128]{2,1,0:T(8,128)(2,1)S(1)} %collective-permute-done), channel_id=1, source_target_pairs={{0,8},{8,16},{16,24},{24,32},{32,40},{40,48},{48,56},{56,64},{64,7... | collective-permute-start | bytes 196616 | tf_op jit(solution)/shard_map/ppermute | solution.py:17
  12.3 5.0 %collective-permute-start.2 = (bf16[2,128,128]{2,1,0:T(8,128)(2,1)S(1)}, bf16[2,128,128]{2,1,0:T(8,128)(2,1)S(1)}, u32[]{:S(2)}, u32[]{:S(2)}) collective-permute-start(bf16[2,128,128]{2,1,0:T(8,128)(2,1)S(1)} %collective-permute-done.1), channel_id=1, source_target_pairs={{0,8},{8,16},{16,24},{24,32},{32,40},{40,48},{48,56},{56,64},{64,7... | collective-permute-start | bytes 196616 | tf_op jit(solution)/shard_map/ppermute | solution.py:17
  17.3 5.6 %collective-permute-start.3 = (bf16[2,128,128]{2,1,0:T(8,128)(2,1)S(1)}, bf16[2,128,128]{2,1,0:T(8,128)(2,1)S(1)}, u32[]{:S(2)}, u32[]{:S(2)}) collective-permute-start(bf16[2,128,128]{2,1,0:T(8,128)(2,1)S(1)} %collective-permute-done.2), channel_id=1, source_target_pairs={{0,8},{8,16},{16,24},{24,32},{32,40},{40,48},{48,56},{56,64},{64,7... | collective-permute-start | bytes 196616 | tf_op jit(solution)/shard_map/ppermute | solution.py:17
  22.9 10.3 %collective-permute-start.4 = (bf16[2,128,128]{2,1,0:T(8,128)(2,1)S(1)}, bf16[2,128,128]{2,1,0:T(8,128)(2,1)S(1)}, u32[]{:S(2)}, u32[]{:S(2)}) collective-permute-start(bf16[2,128,128]{2,1,0:T(8,128)(2,1)S(1)} %collective-permute-done.3), channel_id=1, source_target_pairs={{0,8},{8,16},{16,24},{24,32},{32,40},{40,48},{48,56},{56,64},{64,7... | collective-permute-start | bytes 196616 | tf_op jit(solution)/shard_map/ppermute | solution.py:17
  33.3 6.2 %collective-permute-start.5 = (bf16[2,128,128]{2,1,0:T(8,128)(2,1)S(1)}, bf16[2,128,128]{2,1,0:T(8,128)(2,1)S(1)}, u32[]{:S(2)}, u32[]{:S(2)}) collective-permute-start(bf16[2,128,128]{2,1,0:T(8,128)(2,1)S(1)} %collective-permute-done.4), channel_id=1, source_target_pairs={{0,8},{8,16},{16,24},{24,32},{32,40},{40,48},{48,56},{56,64},{64,7... | collective-permute-start | bytes 196616 | tf_op jit(solution)/shard_map/ppermute | solution.py:17
  39.5 6.5 %collective-permute-start.6 = (bf16[2,128,128]{2,1,0:T(8,128)(2,1)S(1)}, bf16[2,128,128]{2,1,0:T(8,128)(2,1)S(1)}, u32[]{:S(2)}, u32[]{:S(2)}) collective-permute-start(bf16[2,128,128]{2,1,0:T(8,128)(2,1)S(1)} %collective-permute-done.5), channel_id=1, source_target_pairs={{0,8},{8,16},{16,24},{24,32},{32,40},{40,48},{48,56},{56,64},{64,7... | collective-permute-start | bytes 196616 | tf_op jit(solution)/shard_map/ppermute | solution.py:17
  46.0 5.9 %collective-permute-start.7 = (bf16[2,128,128]{2,1,0:T(8,128)(2,1)S(1)}, bf16[2,128,128]{2,1,0:T(8,128)(2,1)S(1)}, u32[]{:S(2)}, u32[]{:S(2)}) collective-permute-start(bf16[2,128,128]{2,1,0:T(8,128)(2,1)S(1)} %collective-permute-done.6), channel_id=1, source_target_pairs={{0,8},{8,16},{16,24},{24,32},{32,40},{40,48},{48,56},{56,64},{64,7... | collective-permute-start | bytes 196616 | tf_op jit(solution)/shard_map/ppermute | solution.py:17
  53.8 0.5 copy-start.8
  53.9 0.7 copy-start
  61.9 1.8 copy-start.1
  61.9 1.8 copy-start.2
  61.9 1.8 copy-start.4
  63.6 1.0 copy-start.3
  64.5 3.0 copy-start.9
  67.5 0.5 copy-start.8
  67.7 0.7 copy-start
  75.6 1.8 copy-start.1
  75.6 1.8 copy-start.2
  75.6 1.8 copy-start.4
  77.4 1.0 copy-start.3
  78.2 3.0 copy-start.9
  81.2 0.5 copy-start.8
  81.4 0.7 copy-start
  89.4 1.8 copy-start.1
  89.4 1.8 copy-start.2
  89.4 1.8 copy-start.4
  91.1 1.0 copy-start.3
  92.0 3.0 copy-start.9
  95.0 6.0 %collective-permute-start.8 = (f32[2,128,128]{2,1,0:T(8,128)S(1)}, f32[2,128,128]{2,1,0:T(8,128)S(1)}, u32[]{:S(2)}, u32[]{:S(2)}) collective-permute-start(f32[2,128,128]{2,1,0:T(8,128)S(1)} %fusion.33), channel_id=1, source_target_pairs={{8,0},{16,8},{24,16},{32,24},{40,32},{48,40},{56,48},{64,56},{72,6... | collective-permute-start | bytes 393224 | tf_op jit(solution)/shard_map/ppermute | solution.py:17
  101.1 6.0 %collective-permute-start.9 = (f32[2,128,128]{2,1,0:T(8,128)S(1)}, f32[2,128,128]{2,1,0:T(8,128)S(1)}, u32[]{:S(2)}, u32[]{:S(2)}) collective-permute-start(f32[2,128,128]{2,1,0:T(8,128)S(1)} %fusion.35), channel_id=1, source_target_pairs={{8,0},{16,8},{24,16},{32,24},{40,32},{48,40},{56,48},{64,56},{72,6... | collective-permute-start | bytes 393224 | tf_op jit(solution)/shard_map/ppermute | solution.py:17
  107.1 7.0 %collective-permute-start.10 = (f32[2,128,128]{2,1,0:T(8,128)S(1)}, f32[2,128,128]{2,1,0:T(8,128)S(1)}, u32[]{:S(2)}, u32[]{:S(2)}) collective-permute-start(f32[2,128,128]{2,1,0:T(8,128)S(1)} %fusion.37), channel_id=1, source_target_pairs={{8,0},{16,8},{24,16},{32,24},{40,32},{48,40},{56,48},{64,56},{72,6... | collective-permute-start | bytes 393224 | tf_op jit(solution)/shard_map/ppermute | solution.py:17
  114.1 7.2 %collective-permute-start.11 = (f32[2,128,128]{2,1,0:T(8,128)S(1)}, f32[2,128,128]{2,1,0:T(8,128)S(1)}, u32[]{:S(2)}, u32[]{:S(2)}) collective-permute-start(f32[2,128,128]{2,1,0:T(8,128)S(1)} %fusion.39), channel_id=1, source_target_pairs={{8,0},{16,8},{24,16},{32,24},{40,32},{48,40},{56,48},{64,56},{72,6... | collective-permute-start | bytes 393224 | tf_op jit(solution)/shard_map/ppermute | solution.py:17
  121.3 22.5 %copy-start.5 = (f32[3,128,4,128]{3,1,2,0:T(8,128)S(1)}, f32[3,128,4,128]{3,1,2,0:T(8,128)}, u32[]{:S(2)}) copy-start(f32[3,128,4,128]{3,1,2,0:T(8,128)} %get-tuple-element.53) | copy-start | bytes 2359300
  121.3 7.1 %collective-permute-start.12 = (f32[2,128,128]{2,1,0:T(8,128)S(1)}, f32[2,128,128]{2,1,0:T(8,128)S(1)}, u32[]{:S(2)}, u32[]{:S(2)}) collective-permute-start(f32[2,128,128]{2,1,0:T(8,128)S(1)} %fusion.41), channel_id=1, source_target_pairs={{8,0},{16,8},{24,16},{32,24},{40,32},{48,40},{56,48},{64,56},{72,6... | collective-permute-start | bytes 393224 | tf_op jit(solution)/shard_map/ppermute | solution.py:17
  128.4 6.9 %collective-permute-start.13 = (f32[2,128,128]{2,1,0:T(8,128)S(1)}, f32[2,128,128]{2,1,0:T(8,128)S(1)}, u32[]{:S(2)}, u32[]{:S(2)}) collective-permute-start(f32[2,128,128]{2,1,0:T(8,128)S(1)} %fusion.43), channel_id=1, source_target_pairs={{8,0},{16,8},{24,16},{32,24},{40,32},{48,40},{56,48},{64,56},{72,6... | collective-permute-start | bytes 393224 | tf_op jit(solution)/shard_map/ppermute | solution.py:17
  135.4 7.2 %collective-permute-start.14 = (f32[2,128,128]{2,1,0:T(8,128)S(1)}, f32[2,128,128]{2,1,0:T(8,128)S(1)}, u32[]{:S(2)}, u32[]{:S(2)}) collective-permute-start(f32[2,128,128]{2,1,0:T(8,128)S(1)} %fusion.45), channel_id=1, source_target_pairs={{8,0},{16,8},{24,16},{32,24},{40,32},{48,40},{56,48},{64,56},{72,6... | collective-permute-start | bytes 393224 | tf_op jit(solution)/shard_map/ppermute | solution.py:17
  142.6 8.9 %collective-permute-start.15 = (f32[2,128,128]{2,1,0:T(8,128)S(1)}, f32[2,128,128]{2,1,0:T(8,128)S(1)}, u32[]{:S(2)}, u32[]{:S(2)}) collective-permute-start(f32[2,128,128]{2,1,0:T(8,128)S(1)} %fusion.32), channel_id=1, source_target_pairs={{8,0},{16,8},{24,16},{32,24},{40,32},{48,40},{56,48},{64,56},{72,6... | collective-permute-start | bytes 393224 | tf_op jit(solution)/shard_map/ppermute | solution.py:17
where the time goes:
time: 354 us; the launch traced here: 353 us
  blocking collectives  196 us (55%)
  waiting for transfers between devices  53.7 us (15%)
  starting transfers between devices  46.2 us (13%)
  matrix products  26.6 us (8%)
  local copies, waits for them, and re-layouts  20.3 us (6%)
  other arithmetic  5.46 us (2%)
  between operations  4.04 us (1%)
    psum x1, blocking collectives, local(): total = lax.psum(local_squares, ('ctx', 'head'))  196 us
    ppermute x16, waiting for transfers between devices, passed_along(): lax.ppermute(value, axis, [(source, source + steps) for source in range(l...  53.7 us
    ppermute x16, starting transfers between devices, passed_along(): lax.ppermute(value, axis, [(source, source + steps) for source in range(l...  46.2 us
    dynamic_slice x6, local copies, waits for them, and re-layouts, local(): (dk_total, dv_total), grad_query = lax.scan(stepper, (zeros, zeros), inputs)  9.72 us
  transfers between devices with their start and end apart: 16, of which 15 were waited for; matrix products, arithmetic and copies ran while one was open for 2% of the time, Pallas kernels for 0%

commit v1 on v0

v1 whole, which is shorter than its diff:
```python
from functools import partial
import math

import jax
import jax.numpy as jnp
from jax import lax
from jax.experimental import pallas as pl
from jax.experimental.pallas import tpu as pltpu
from jax.sharding import PartitionSpec as P

HD = 128
LOG2E = 1.4426950408889634
MASKED = -1e30
MESH = pl.DeviceIdType.MESH
F32 = jnp.float32
BF16 = jnp.bfloat16
PIECE = 128


def nn(a, b):
    return lax.dot_general(a, b, (((1,), (0,)), ((), ())), preferred_element_type=F32)


def kernel(
    sizes, scale, count_all,
    doc_ref, q_ref, k_ref, v_ref, do_ref,
    dq_ref, dk_ref, dv_ref, rms_ref,
    kv, kt, qt, dot_, qs, dos, p_buf, dp_buf, ds_buf, pb_buf, dqt,
    m_all, l_row, r_row, g_out, g_in,
    sum_head, sum_lo, sum_hi,
    kv_send, kv_recv, g_send, g_recv, s_send, s_recv,
):
    n_ctx, n_head, n_lo, reach, docs = sizes
    n_hi = n_ctx // n_lo
    tok = q_ref.shape[0]
    heads = q_ref.shape[1] // HD
    wide = heads * tok
    pieces = 2 * tok // PIECE
    me = lax.axis_index("ctx")
    mh = lax.axis_index("head")
    right = lax.rem(me + 1, n_ctx)
    left = lax.rem(me + n_ctx - 1, n_ctx)
    my_lo = lax.rem(me, n_lo)
    my_hi = lax.div(me, n_lo)

    def head_partner(i):
        return {"head": lax.rem(mh + i, n_head)}

    def lo_partner(i):
        return {"ctx": my_hi * n_lo + lax.rem(my_lo + i, n_lo)}

    def hi_partner(i):
        return {"ctx": lax.rem(my_hi + i, n_hi) * n_lo + my_lo}

    barrier = pltpu.get_barrier_semaphore()
    pl.semaphore_signal(barrier, inc=1, device_id={"ctx": right}, device_id_type=MESH)
    pl.semaphore_signal(barrier, inc=1, device_id={"ctx": left}, device_id_type=MESH)
    for partner, n in ((head_partner, n_head), (lo_partner, n_lo), (hi_partner, n_hi)):

        def greet(i, carry, partner=partner):
            pl.semaphore_signal(barrier, inc=1, device_id=partner(i), device_id_type=MESH)
            return carry

        lax.fori_loop(1, n, greet, 0)

    kv[0, 0:tok, :] = k_ref[...]
    kv[0, tok : 2 * tok, :] = v_ref[...]
    for h in range(heads):
        cols = slice(h * HD, (h + 1) * HD)
        rows = slice(h * tok, (h + 1) * tok)
        qs[rows, :] = q_ref[:, cols]
        dos[rows, :] = do_ref[:, cols]
        qt[:, rows] = q_ref[:, cols].T
        dot_[:, rows] = do_ref[:, cols].T

    pos = me * tok + lax.broadcasted_iota(jnp.int32, (8, tok), 1)
    first = jnp.zeros((8, tok), jnp.int32)
    begin = jnp.int32(0)
    for i in range(docs):
        first = jnp.where(begin <= pos, begin, first)
        begin = begin + doc_ref[i]
    first = first[0:1]
    pos = pos[0:1]

    pl.semaphore_wait(barrier, 2 + (n_head - 1) + (n_lo - 1) + (n_hi - 1))

    def kv_copy(d, i):
        rows = pl.ds(i * PIECE, PIECE)
        return pltpu.make_async_remote_copy(
            src_ref=kv.at[d, rows],
            dst_ref=kv.at[d + 1, rows],
            send_sem=kv_send.at[d, i],
            recv_sem=kv_recv.at[d, i],
            device_id={"ctx": right},
            device_id_type=MESH,
        )

    def g_copy(d, i):
        rows = pl.ds(i * PIECE, PIECE)
        return pltpu.make_async_remote_copy(
            src_ref=g_out.at[d, rows],
            dst_ref=g_in.at[d, rows],
            send_sem=g_send.at[d, i],
            recv_sem=g_recv.at[d, i],
            device_id={"ctx": left},
            device_id_type=MESH,
        )

    chunk = 256
    chunks = [slice(j, j + chunk) for j in range(0, wide, chunk)]

    def scores_of(d, opening):
        key = (me - d) * tok + lax.broadcasted_iota(jnp.int32, (tok, tok), 0)
        fine = (key >= first) & (key <= pos)
        bias = jnp.where(fine, 0.0, MASKED)
        bias = jnp.concatenate([bias] * (chunk // tok), axis=1)
        k_d = kv[d, 0:tok, :]
        v_d = kv[d, tok : 2 * tok, :]
        kt[d] = k_d.T
        for cols in chunks:
            s = nn(k_d, qt[:, cols]) * (scale * LOG2E) + bias
            top = jnp.max(s, axis=0, keepdims=True)
            if opening:
                m_new = top
            else:
                m_old = m_all[d - 1, :, cols]
                m_new = jnp.maximum(m_old, top)
            p = jnp.exp2(s - m_new)
            dp = nn(v_d, dot_[:, cols])
            p_buf[d, :, cols] = p
            dp_buf[d, :, cols] = dp
            l_add = jnp.sum(p, axis=0, keepdims=True)
            r_add = jnp.sum(p * dp, axis=0, keepdims=True)
            if not opening:
                shrink = jnp.exp2(m_old - m_new)
                l_add = l_add + shrink * l_row[:, cols]
                r_add = r_add + shrink * r_row[:, cols]
            m_all[d, :, cols] = m_new
            l_row[:, cols] = l_add
            r_row[:, cols] = r_add

    for i in range(pieces):
        kv_copy(0, i).start()
    scores_of(0, True)

    def gather_step(d, carry):
        for i in range(pieces):
            kv_copy(d - 1, i).wait_recv()

            @pl.when(d < reach)
            def _(i=i):
                kv_copy(d, i).start()

        scores_of(d, False)
        return carry

    lax.fori_loop(1, reach + 1, gather_step, 0)

    inverse = 1.0 / l_row[...]
    l_row[...] = inverse
    r_row[...] = r_row[...] * inverse

    def grads_of(d):
        for cols in chunks:
            factor = jnp.exp2(m_all[d, :, cols] - m_all[reach, :, cols]) * l_row[:, cols]
            w = p_buf[d, :, cols] * factor
            pb_buf[:, cols] = w.astype(BF16)
            ds_buf[:, cols] = (w * (dp_buf[d, :, cols] - r_row[:, cols])).astype(BF16)
        dk = nn(ds_buf[...], qs[...]) * scale
        dv = nn(pb_buf[...], dos[...])
        return dk, dv

    def queries_of(d, opening):
        for cols in chunks:
            part = nn(kt[d], ds_buf[:, cols])
            if opening:
                dqt[:, cols] = part
            else:
                dqt[:, cols] = dqt[:, cols] + part

    def send_back(d):
        for i in range(pieces):
            g_copy(d, i).start()

    dk, dv = grads_of(reach)
    g_out[reach, 0:tok, :] = dk.astype(BF16)
    g_out[reach, tok : 2 * tok, :] = dv.astype(BF16)
    send_back(reach)
    queries_of(reach, True)

    def return_step(step, carry):
        d = reach - step
        dk, dv = grads_of(d)
        for i in range(pieces):
            g_copy(d + 1, i).wait_recv()
        g_out[d, 0:tok, :] = (dk + g_in[d + 1, 0:tok, :].astype(F32)).astype(BF16)
        g_out[d, tok : 2 * tok, :] = (dv + g_in[d + 1, tok : 2 * tok, :].astype(F32)).astype(BF16)
        send_back(d)
        queries_of(d, False)
        return carry

    lax.fori_loop(1, reach, return_step, 0)
    dk, dv = grads_of(0)
    queries_of(0, False)
    squares = jnp.zeros((8, HD), F32)
    for h in range(heads):
        part = dqt[:, h * tok : (h + 1) * tok] * scale
        squares = squares + jnp.sum((part * part).reshape(HD // 8, 8, tok), axis=0)
        dq_ref[:, h * HD : (h + 1) * HD] = part.T.astype(BF16)
    for i in range(pieces):
        g_copy(1, i).wait_recv()
    dk = dk + g_in[1, 0:tok, :].astype(F32)
    dv = dv + g_in[1, tok : 2 * tok, :].astype(F32)
    both = dk * dk + dv * dv
    squares = squares + jnp.sum(both.reshape(tok // 8, 8, HD), axis=0)

    sends = 0
    for level, (partner, n, mine, slots) in enumerate((
        (head_partner, n_head, mh, sum_head),
        (lo_partner, n_lo, my_lo, sum_lo),
        (hi_partner, n_hi, my_hi, sum_hi),
    )):
        slots[mine] = squares

        def push(i, carry, partner=partner, mine=mine, slots=slots, level=level):
            pltpu.make_async_remote_copy(
                src_ref=slots.at[mine],
                dst_ref=slots.at[mine],
                send_sem=s_send.at[level],
                recv_sem=s_recv.at[level],
                device_id=partner(i),
                device_id_type=MESH,
            ).start()
            return carry

        lax.fori_loop(1, n, push, 0)
        if level == 0:
            dk_ref[...] = dk.astype(BF16)
            dv_ref[...] = dv.astype(BF16)
        if n == 1:
            continue
        others = slots.at[pl.ds(0, n - 1)]
        pltpu.make_async_copy(others, others, s_recv.at[level]).wait()
        squares = slots[0]
        for i in range(1, n):
            squares = squares + slots[i]
    rms_ref[...] = jnp.broadcast_to(jnp.sqrt(jnp.sum(squares) / count_all), rms_ref.shape)

    for level, (n, slots) in enumerate(((n_head, sum_head), (n_lo, sum_lo), (n_hi, sum_hi))):
        if n == 1:
            continue
        others = slots.at[pl.ds(0, n - 1)]
        pltpu.make_async_copy(others, others, s_send.at[level]).wait()
    for d in range(reach):
        for i in range(pieces):
            kv_copy(d, i).wait_send()
            g_copy(d + 1, i).wait_send()


def local(mesh_sizes, queries, keys, values, out_grad, doc_lengths):
    n_ctx, n_head = mesh_sizes
    tok, q_cols = queries.shape
    wide = q_cols // HD * tok
    n_lo = min(8, n_ctx)
    reach = min(8, n_ctx // 2)
    docs = doc_lengths.shape[0]
    count_all = n_ctx * tok * n_head * (q_cols + 2 * HD)
    pieces = 2 * tok // PIECE
    vmem = pl.BlockSpec(memory_space=pltpu.VMEM)
    dq, dk, dv, rms = pl.pallas_call(
        partial(kernel, (n_ctx, n_head, n_lo, reach, docs), HD ** (-0.5), float(count_all)),
        out_shape=(
            jax.ShapeDtypeStruct((tok, q_cols), BF16),
            jax.ShapeDtypeStruct((tok, HD), BF16),
            jax.ShapeDtypeStruct((tok, HD), BF16),
            jax.ShapeDtypeStruct((8, HD), F32),
        ),
        in_specs=[pl.BlockSpec(memory_space=pltpu.SMEM)] + [vmem] * 4,
        out_specs=(vmem,) * 4,
        scratch_shapes=[
            pltpu.VMEM((reach + 1, 2 * tok, HD), BF16),
            pltpu.VMEM((reach + 1, HD, tok), BF16),
            pltpu.VMEM((HD, wide), BF16),
            pltpu.VMEM((HD, wide), BF16),
            pltpu.VMEM((wide, HD), BF16),
            pltpu.VMEM((wide, HD), BF16),
            pltpu.VMEM((reach + 1, tok, wide), F32),
            pltpu.VMEM((reach + 1, tok, wide), F32),
            pltpu.VMEM((tok, wide), BF16),
            pltpu.VMEM((tok, wide), BF16),
            pltpu.VMEM((HD, wide), F32),
            pltpu.VMEM((reach + 1, 1, wide), F32),
            pltpu.VMEM((1, wide), F32),
            pltpu.VMEM((1, wide), F32),
            pltpu.VMEM((reach + 1, 2 * tok, HD), BF16),
            pltpu.VMEM((reach + 1, 2 * tok, HD), BF16),
            pltpu.VMEM((n_head, 8, HD), F32),
            pltpu.VMEM((n_lo, 8, HD), F32),
            pltpu.VMEM((n_ctx // n_lo, 8, HD), F32),
            pltpu.SemaphoreType.DMA((reach + 1, pieces)),
            pltpu.SemaphoreType.DMA((reach + 1, pieces)),
            pltpu.SemaphoreType.DMA((reach + 1, pieces)),
            pltpu.SemaphoreType.DMA((reach + 1, pieces)),
            pltpu.SemaphoreType.DMA((3,)),
            pltpu.SemaphoreType.DMA((3,)),
        ],
        compiler_params=pltpu.CompilerParams(
            collective_id=0, has_side_effects=True, vmem_limit_bytes=40 * 1024 * 1024
        ),
        cost_estimate=pl.CostEstimate(
            flops=10 * wide * (reach + 1) * tok * HD,
            bytes_accessed=2 * 3 * tok * q_cols,
            transcendentals=wide * (reach + 1) * tok,
        ),
    )(doc_lengths, queries, keys, values, out_grad)
    return dq, dk, dv, rms[0, 0]


def solution(mesh):
    sizes = (mesh.shape["ctx"], mesh.shape["head"])
    return jax.shard_map(
        partial(local, sizes),
        mesh=mesh,
        in_specs=(P("ctx", "head"), P("ctx", "head"), P("ctx", "head"), P("ctx", "head"), P()),
        out_specs=(P("ctx", "head"), P("ctx", "head"), P("ctx", "head"), P()),
        check_vma=False,
    )
```

time: 354 us -> 116 us (0.33)
  blocking collectives: 196 us -> 0 us
  Pallas kernels: 0 us -> 108 us
  waiting for transfers between devices: 53.7 us -> 0 us
  starting transfers between devices: 46.2 us -> 0 us
  matrix products: 26.6 us -> 0 us
  local copies, waits for them, and re-layouts: 20.3 us -> 6.64 us
  other arithmetic: 5.46 us -> 0 us
    psum x1 -> x0, blocking collectives: 196 us -> none  [local(): total = lax.psum(local_squares, ('ctx', 'head'))]
    pallas_call x0 -> x1, Pallas kernels: none -> 108 us  [local(): pl.pallas_call(partial(kernel, (n_ctx, n_head, n_lo, reach, docs), HD **...]
    ppermute x16 -> x0, waiting for transfers between devices: 53.7 us -> none  [passed_along(): lax.ppermute(value, axis, [(source, source + steps) for source in range(l...]
    ppermute x16 -> x0, starting transfers between devices: 46.2 us -> none  [passed_along(): lax.ppermute(value, axis, [(source, source + steps) for source in range(l...]
    dot_general x18 -> x0, matrix products: 26.6 us -> none  [the longest x3 5.33 us: head_group(): jnp.einsum('gqk,qgd->kd', weights_low, grad_part, preferred_element_type=...]
    dynamic_slice x6 -> x0, local copies, waits for them, and re-layouts: 9.72 us -> none  [local(): (dk_total, dv_total), grad_query = lax.scan(stepper, (zeros, zeros), inputs)]
  transfers between devices with their start and end apart: 16 -> 0, of which waited for: 15 -> 0; matrix products, arithmetic and copies ran while one was open for 2% -> 0% of each run, Pallas kernels for 0% -> 0%
where the time goes in v1:
time: 116 us
  Pallas kernels  108 us (93%)
  local copies, waits for them, and re-layouts  6.64 us (6%)
    pallas_call x1, Pallas kernels, local(): pl.pallas_call(partial(kernel, (n_ctx, n_head, n_lo, reach, docs), HD **...  108 us
    unnamed x13, local copies, waits for them, and re-layouts  6.13 us

profile of v1, /device:TPU:1, one launch (start us, length us, event | category | flops | bytes accessed | tf_op | source)
XLA Modules:
  0.0 115.8 jit_solution(3187863369265737657)
XLA Ops:
  0.6 0.0 copy-start
  0.6 1.0 copy-done
  1.6 0.0 copy-start.1
  1.6 1.0 copy-done.1
  2.6 0.0 copy-start.2
  2.6 0.8 copy-done.2
  3.4 0.0 copy-start.3
  3.4 0.8 copy-done.3
  4.1 0.0 copy-start.4
  4.1 0.7 copy-done.4
  4.8 108.5 %shard_map.84 = (bf16[128,1536]{1,0:T(8,128)(2,1)S(1)}, bf16[128,128]{1,0:T(8,128)(2,1)S(1)}, bf16[128,128]{1,0:T(8,128)(2,1)S(1)}, f32[8,128]{1,0:T(8,128)S(1)}) custom-call(s32[32]{0:T(128)S(1)} %copy-done.4, bf16[128,1536]{1,0:T(8,128)(2,1)S(1)} %copy-done, bf16[128,128]{1,0:T(8,128)(2,1)S(1)} %copy-done.2, bf16[128,128]{1,0:T(8,128)(2,1)S(1)} %copy-done.3, ...), custom_call_target="tpu_custom_call" | custom-call | flops 2264924160 | bytes 1179648 | tf_op jit(solution)/shard_map/pallas_call | solution.py:270
  113.3 0.5 slice.3
  113.8 0.7 copy.12
  114.6 0.6 copy.13
  115.2 0.6 copy.14
Async XLA Ops:
  0.6 1.0 copy-start
  1.6 1.0 copy-start.1
  2.6 0.8 copy-start.2
  3.4 0.8 copy-start.3
  4.1 0.7 copy-start.4

commit v2 on v1

v2 whole, which is shorter than its diff:
```python
from functools import partial

import jax
import jax.numpy as jnp
from jax import lax
from jax.experimental import pallas as pl
from jax.experimental.pallas import tpu as pltpu
from jax.sharding import PartitionSpec as P

HD = 128
LOG2E = 1.4426950408889634
MASKED = -1e30
MESH = pl.DeviceIdType.MESH
F32 = jnp.float32
BF16 = jnp.bfloat16
PIECE = 64
HOP = 5


def nn(a, b):
    return lax.dot_general(a, b, (((1,), (0,)), ((), ())), preferred_element_type=F32)


def kernel(
    sizes, scale, count_all,
    doc_ref, q_hbm, k_hbm, v_hbm, do_hbm,
    dq_ref, dk_ref, dv_ref, rms_ref,
    kv, kt, q_ref, do_ref, qt, dot_, qs, dos, p_buf, dp_buf, ds_buf, pb_buf, dqt,
    m_all, m_row, l_row, r_row, g_out, g_in,
    sum_head, sum_x, sum_z,
    load_sem, kv_send, kv_recv, g_send, g_recv, s_send, s_recv, known_sem,
):
    n_x, n_z, n_head, docs = sizes
    n_ctx = n_x * n_z
    tok = q_ref.shape[0]
    heads = q_ref.shape[1] // HD
    wide = heads * tok
    pieces = 2 * tok // PIECE
    me = lax.axis_index("ctx")
    mh = lax.axis_index("head")
    my_x = lax.div(me, n_z)
    my_z = lax.rem(me, n_z)

    def ring(step):
        return {"ctx": lax.rem(me + (step + n_ctx), n_ctx)}

    def head_partner(i):
        return {"head": lax.rem(mh + i, n_head)}

    def x_partner(i):
        return {"ctx": lax.rem(my_x + i, n_x) * n_z + my_z}

    def z_partner(i):
        return {"ctx": my_x * n_z + lax.rem(my_z + (i + n_z), n_z)}

    def tell(sem, partner):
        pl.semaphore_signal(sem, inc=1, device_id=partner, device_id_type=MESH)

    def load(i, source, target):
        return pltpu.make_async_copy(source, target, load_sem.at[i])

    loads = (
        load(0, k_hbm, kv.at[0, pl.ds(0, tok)]),
        load(1, v_hbm, kv.at[0, pl.ds(tok, tok)]),
        load(2, q_hbm, q_ref),
        load(3, do_hbm, do_ref),
    )
    for copy in loads:
        copy.start()

    barrier = pltpu.get_barrier_semaphore()
    near = [ring(1), ring(HOP), ring(-1), ring(-HOP)]
    near += [z_partner(1), z_partner(-1), z_partner(2), z_partner(-2)]
    near += [x_partner(i) for i in range(1, n_x)] + [head_partner(i) for i in range(1, n_head)]
    for partner in near:
        tell(barrier, partner)
    loads[0].wait()
    loads[1].wait()
    pl.semaphore_wait(barrier, len(near))

    def kv_copy(source, to, step, i):
        rows = pl.ds(i * PIECE, PIECE)
        return pltpu.make_async_remote_copy(
            src_ref=kv.at[source, rows],
            dst_ref=kv.at[to, rows],
            send_sem=kv_send.at[to, i],
            recv_sem=kv_recv.at[to, i],
            device_id=ring(step),
            device_id_type=MESH,
        )

    def g_copy(d, step, i):
        rows = pl.ds(i * PIECE, PIECE)
        return pltpu.make_async_remote_copy(
            src_ref=g_out.at[d, rows],
            dst_ref=g_in.at[d, rows],
            send_sem=g_send.at[d, i],
            recv_sem=g_recv.at[d, i],
            device_id=ring(step),
            device_id_type=MESH,
        )

    for i in range(pieces):
        kv_copy(0, HOP, HOP, i).start()
    for i in range(pieces):
        kv_copy(0, 1, 1, i).start()

    spans = []
    while (2 << len(spans)) < n_z // 2:
        spans.append(2 << len(spans))

    def tell_known(r):
        if r < len(spans):
            tell(known_sem.at[r], z_partner(spans[r]))
            tell(known_sem.at[r], z_partner(-spans[r]))

    def hear_known(r):
        if r < len(spans):
            pl.semaphore_wait(known_sem.at[r], 2)

    tell_known(0)

    pos = me * tok + lax.broadcasted_iota(jnp.int32, (8, tok), 1)
    first = jnp.zeros((8, tok), jnp.int32)
    begin = jnp.int32(0)
    for i in range(docs):
        first = jnp.where(begin <= pos, begin, first)
        begin = begin + doc_ref[i]
    first = first[0:1]
    pos = pos[0:1]

    loads[2].wait()
    loads[3].wait()
    for h in range(heads):
        cols = slice(h * HD, (h + 1) * HD)
        rows = slice(h * tok, (h + 1) * tok)
        qs[rows, :] = q_ref[:, cols]
        dos[rows, :] = do_ref[:, cols]
        qt[:, rows] = q_ref[:, cols].T
        dot_[:, rows] = do_ref[:, cols].T

    chunk = 256
    chunks = [slice(j, j + chunk) for j in range(0, wide, chunk)]

    def scores_of(d, opening):
        key = (me - d) * tok + lax.broadcasted_iota(jnp.int32, (tok, tok), 0)
        fine = (key >= first) & (key <= pos)
        bias = jnp.where(fine, 0.0, MASKED)
        bias = jnp.concatenate([bias] * (chunk // tok), axis=1)
        k_d = kv[d, 0:tok, :]
        v_d = kv[d, tok : 2 * tok, :]
        kt[d] = k_d.T
        for cols in chunks:
            s = nn(k_d, qt[:, cols]) * (scale * LOG2E) + bias
            top = jnp.max(s, axis=0, keepdims=True)
            if opening:
                m_new = top
            else:
                m_old = m_row[:, cols]
                m_new = jnp.maximum(m_old, top)
            p = jnp.exp2(s - m_new)
            dp = nn(v_d, dot_[:, cols])
            p_buf[d, :, cols] = p
            dp_buf[d, :, cols] = dp
            l_add = jnp.sum(p, axis=0, keepdims=True)
            r_add = jnp.sum(p * dp, axis=0, keepdims=True)
            if not opening:
                shrink = jnp.exp2(m_old - m_new)
                l_add = l_add + shrink * l_row[:, cols]
                r_add = r_add + shrink * r_row[:, cols]
            m_all[d, :, cols] = m_new
            m_row[:, cols] = m_new
            l_row[:, cols] = l_add
            r_row[:, cols] = r_add

    scores_of(0, True)

    def gather_step(j, carry):
        for d in (j, j + HOP - 1):
            for i in range(pieces):
                kv_copy(0, d, 1, i).wait_recv()

                @pl.when(j < HOP - 1)
                def _(d=d, i=i):
                    kv_copy(d, d + 1, 1, i).start()

            scores_of(d, False)
        return carry

    lax.fori_loop(1, HOP, gather_step, 0)
    hear_known(0)

    inverse = 1.0 / l_row[...]
    l_row[...] = inverse
    r_row[...] = r_row[...] * inverse

    def grads_of(d, at):
        for cols in chunks:
            factor = jnp.exp2(m_all[d, :, cols] - m_row[:, cols]) * l_row[:, cols]
            w = p_buf[d, :, cols] * factor
            pb_buf[at, :, cols] = w.astype(BF16)
            ds_buf[at, :, cols] = (w * (dp_buf[d, :, cols] - r_row[:, cols])).astype(BF16)
        dk = nn(ds_buf[at], qs[...]) * scale
        dv = nn(pb_buf[at], dos[...])
        return dk, dv

    def queries_of(d, at, opening):
        for cols in chunks:
            part = nn(kt[d], ds_buf[at, :, cols])
            if opening:
                dqt[:, cols] = part
            else:
                dqt[:, cols] = dqt[:, cols] + part

    def piece_of(dk, dv, i):
        whole, begin = (dk, i * PIECE) if i * PIECE < tok else (dv, i * PIECE - tok)
        return whole[begin : begin + PIECE]

    def return_pair(j, opening, last):
        far, close = 2 * (HOP - 1) - j, HOP - 1 - j
        for at, d in enumerate((far, close)):
            dk, dv = grads_of(d, at)
            step = -HOP if last and at == 0 else -1
            for i in range(pieces):
                rows = slice(i * PIECE, (i + 1) * PIECE)
                part = piece_of(dk, dv, i)
                if not opening:
                    g_copy(d + 1, -1, i).wait_recv()
                    part = part + g_in[d + 1, rows, :].astype(F32)
                g_out[d, rows, :] = part.astype(BF16)
                g_copy(d, step, i).start()
        queries_of(far, 0, opening)
        queries_of(close, 1, False)

    return_pair(0, True, False)
    tell_known(1)

    def return_step(j, carry):
        return_pair(j, False, False)
        return carry

    lax.fori_loop(1, HOP - 2, return_step, 0)
    return_pair(HOP - 2, False, True)
    hear_known(1)
    tell_known(2)
    dk, dv = grads_of(0, 0)
    queries_of(0, 0, False)
    squares = jnp.zeros((8, HD), F32)
    for h in range(heads):
        part = dqt[:, h * tok : (h + 1) * tok] * scale
        squares = squares + jnp.sum((part * part).reshape(HD // 8, 8, tok), axis=0)
        dq_ref[:, h * HD : (h + 1) * HD] = part.T.astype(BF16)
    hear_known(2)
    for i in range(pieces):
        rows = slice(i * PIECE, (i + 1) * PIECE)
        g_copy(1, -1, i).wait_recv()
        g_copy(HOP, -HOP, i).wait_recv()
        part = piece_of(dk, dv, i) + g_in[1, rows, :].astype(F32) + g_in[HOP, rows, :].astype(F32)
        squares = squares + jnp.sum((part * part).reshape(PIECE // 8, 8, HD), axis=0)
        out, begin = (dk_ref, i * PIECE) if i * PIECE < tok else (dv_ref, i * PIECE - tok)
        out[begin : begin + PIECE, :] = part.astype(BF16)

    levels = (
        (head_partner, range(1, n_head), mh, sum_head),
        (x_partner, range(1, n_x), my_x, sum_x),
        (z_partner, sorted(range(1, n_z), key=lambda i: -min(i, n_z - i)), my_z, sum_z),
    )
    for level, (partner, offsets, mine, slots) in enumerate(levels):
        n = slots.shape[0]
        slots[mine] = squares
        for i in offsets:
            pltpu.make_async_remote_copy(
                src_ref=slots.at[mine],
                dst_ref=slots.at[mine],
                send_sem=s_send.at[level],
                recv_sem=s_recv.at[level],
                device_id=partner(i),
                device_id_type=MESH,
            ).start()
        if n > 1:
            others = slots.at[pl.ds(0, n - 1)]
            pltpu.make_async_copy(others, others, s_recv.at[level]).wait()
        squares = slots[0]
        for i in range(1, n):
            squares = squares + slots[i]
    rms_ref[...] = jnp.broadcast_to(jnp.sqrt(jnp.sum(squares) / count_all), rms_ref.shape)

    for level, (_, _, _, slots) in enumerate(levels):
        n = slots.shape[0]
        if n > 1:
            others = slots.at[pl.ds(0, n - 1)]
            pltpu.make_async_copy(others, others, s_send.at[level]).wait()
    for d in range(1, 2 * HOP - 1):
        for i in range(pieces):
            kv_copy(0, d, 1, i).wait_send()
            g_copy(d, -1, i).wait_send()


def local(mesh_sizes, queries, keys, values, out_grad, doc_lengths):
    n_ctx, n_head = mesh_sizes
    tok, q_cols = queries.shape
    wide = q_cols // HD * tok
    n_x = 4 if n_ctx == 128 else 2
    n_z = n_ctx // n_x
    blocks = 2 * (HOP - 1) + 1
    docs = doc_lengths.shape[0]
    count_all = n_ctx * tok * n_head * (q_cols + 2 * HD)
    pieces = 2 * tok // PIECE
    vmem = pl.BlockSpec(memory_space=pltpu.VMEM)
    dq, dk, dv, rms = pl.pallas_call(
        partial(kernel, (n_x, n_z, n_head, docs), HD ** (-0.5), float(count_all)),
        out_shape=(
            jax.ShapeDtypeStruct((tok, q_cols), BF16),
            jax.ShapeDtypeStruct((tok, HD), BF16),
            jax.ShapeDtypeStruct((tok, HD), BF16),
            jax.ShapeDtypeStruct((8, HD), F32),
        ),
        in_specs=[pl.BlockSpec(memory_space=pltpu.SMEM)] + [pl.BlockSpec(memory_space=pl.ANY)] * 4,
        out_specs=(vmem,) * 4,
        scratch_shapes=[
            pltpu.VMEM((blocks, 2 * tok, HD), BF16),
            pltpu.VMEM((blocks, HD, tok), BF16),
            pltpu.VMEM((tok, q_cols), BF16),
            pltpu.VMEM((tok, q_cols), BF16),
            pltpu.VMEM((HD, wide), BF16),
            pltpu.VMEM((HD, wide), BF16),
            pltpu.VMEM((wide, HD), BF16),
            pltpu.VMEM((wide, HD), BF16),
            pltpu.VMEM((blocks, tok, wide), F32),
            pltpu.VMEM((blocks, tok, wide), F32),
            pltpu.VMEM((2, tok, wide), BF16),
            pltpu.VMEM((2, tok, wide), BF16),
            pltpu.VMEM((HD, wide), F32),
            pltpu.VMEM((blocks, 1, wide), F32),
            pltpu.VMEM((1, wide), F32),
            pltpu.VMEM((1, wide), F32),
            pltpu.VMEM((1, wide), F32),
            pltpu.VMEM((blocks, 2 * tok, HD), BF16),
            pltpu.VMEM((blocks, 2 * tok, HD), BF16),
            pltpu.VMEM((n_head, 8, HD), F32),
            pltpu.VMEM((n_x, 8, HD), F32),
            pltpu.VMEM((n_z, 8, HD), F32),
            pltpu.SemaphoreType.DMA((4,)),
            pltpu.SemaphoreType.DMA((blocks, pieces)),
            pltpu.SemaphoreType.DMA((blocks, pieces)),
            pltpu.SemaphoreType.DMA((blocks, pieces)),
            pltpu.SemaphoreType.DMA((blocks, pieces)),
            pltpu.SemaphoreType.DMA((3,)),
            pltpu.SemaphoreType.DMA((3,)),
            pltpu.SemaphoreType.REGULAR((3,)),
        ],
        compiler_params=pltpu.CompilerParams(
            collective_id=0, has_side_effects=True, vmem_limit_bytes=56 * 1024 * 1024
        ),
        cost_estimate=pl.CostEstimate(
            flops=10 * wide * blocks * tok * HD,
            bytes_accessed=2 * 3 * tok * q_cols,
            transcendentals=wide * blocks * tok,
        ),
    )(doc_lengths, queries, keys, values, out_grad)
    return dq, dk, dv, rms[0, 0]


def solution(mesh):
    sizes = (mesh.shape["ctx"], mesh.shape["head"])
    return jax.shard_map(
        partial(local, sizes),
        mesh=mesh,
        in_specs=(P("ctx", "head"), P("ctx", "head"), P("ctx", "head"), P("ctx", "head"), P()),
        out_specs=(P("ctx", "head"), P("ctx", "head"), P("ctx", "head"), P()),
        check_vma=False,
    )
```

time: 116 us -> 95.8 us (0.83)
  Pallas kernels: 108 us -> 90.5 us
  local copies, waits for them, and re-layouts: 6.64 us -> 4.35 us
    pallas_call x1, Pallas kernels: 108 us -> 90.5 us  [local(): pl.pallas_call(partial(kernel, (n_x, n_z, n_head, docs), HD ** (-0.5), fl...]
    unnamed x13 -> x7, local copies, waits for them, and re-layouts: 6.13 us -> 3.16 us
where the time goes in v2:
time: 95.8 us; the launch traced here: 95.5 us
  Pallas kernels  90.5 us (94%)
  local copies, waits for them, and re-layouts  4.35 us (5%)
    pallas_call x1, Pallas kernels, local(): pl.pallas_call(partial(kernel, (n_x, n_z, n_head, docs), HD ** (-0.5), fl...  90.5 us
    unnamed x7, local copies, waits for them, and re-layouts  3.16 us

profile of v2, /device:TPU:1, one launch (start us, length us, event | category | flops | bytes accessed | tf_op | source)
XLA Modules:
  0.0 95.5 jit_solution(3263611932960870946)
XLA Ops:
  0.6 90.5 %shard_map.84 = (bf16[128,1536]{1,0:T(8,128)(2,1)}, bf16[128,128]{1,0:T(8,128)(2,1)}, bf16[128,128]{1,0:T(8,128)(2,1)}, f32[8,128]{1,0:T(8,128)}) custom-call(s32[32]{0:T(128)} %doc_ref.1, bf16[128,1536]{1,0:T(8,128)(2,1)} %q_hbm.1, bf16[128,128]{1,0:T(8,128)(2,1)} %k_hbm.1, bf16[128,128]{1,0:T(8,128)(2,1)} %v_hbm.1, bf16[128,1536]{1,0:T(8,128)(2,1)} %do_hbm.1), custom_call_target="tpu_custom_call" | custom-call | flops 2264924160 | bytes 1179648 | tf_op jit(solution)/shard_map/pallas_call | solution.py:310
  91.1 1.2 %slice.3 = f32[1,1]{1,0:T(1,128)} slice(f32[8,128]{1,0:T(8,128)} %get-tuple-element.11), slice={[0:1], [0:1]} | slice | bytes 8 | tf_op jit(solution)/shard_map/slice | solution.py:361
  92.3 0.0 copy-start.1
  92.3 1.8 %copy.12 = bf16[128,1536]{1,0:T(8,128)(2,1)} copy(bf16[128,1536]{1,0:T(8,128)(2,1)} %get-tuple-element.16) | data formatting | bytes 786432
  94.1 0.0 copy-done.1
  94.1 0.0 copy-start
  94.1 0.6 copy.13
  94.7 0.2 copy-done
  94.9 0.6 copy.14
Async XLA Ops:
  92.3 1.8 %copy-start.1 = (bf16[128,128]{1,0:T(8,128)(2,1)S(1)}, bf16[128,128]{1,0:T(8,128)(2,1)}, u32[]{:S(2)}) copy-start(bf16[128,128]{1,0:T(8,128)(2,1)} %get-tuple-element.17) | copy-start | bytes 98308
  94.1 0.8 copy-start

commit v3 on v2

--- a/solution.py
+++ b/solution.py
@@ -27,7 +27,7 @@
     dq_ref, dk_ref, dv_ref, rms_ref,
     kv, kt, q_ref, do_ref, qt, dot_, qs, dos, p_buf, dp_buf, ds_buf, pb_buf, dqt,
     m_all, m_row, l_row, r_row, g_out, g_in,
-    sum_head, sum_x, sum_z,
+    sum_plane, sum_z,
     load_sem, kv_send, kv_recv, g_send, g_recv, s_send, s_recv, known_sem,
 ):
     n_x, n_z, n_head, docs = sizes
@@ -50,6 +50,9 @@
     def x_partner(i):
         return {"ctx": lax.rem(my_x + i, n_x) * n_z + my_z}
 
+    def plane_partner(i):
+        return x_partner(i // n_head) | head_partner(i % n_head)
+
     def z_partner(i):
         return {"ctx": my_x * n_z + lax.rem(my_z + (i + n_z), n_z)}
 
@@ -69,9 +72,9 @@
         copy.start()
 
     barrier = pltpu.get_barrier_semaphore()
-    near = [ring(1), ring(HOP), ring(-1), ring(-HOP)]
-    near += [z_partner(1), z_partner(-1), z_partner(2), z_partner(-2)]
+    near = [ring(-HOP), ring(HOP), ring(-1), ring(1)]
     near += [x_partner(i) for i in range(1, n_x)] + [head_partner(i) for i in range(1, n_head)]
+    near += [z_partner(2), z_partner(-2), z_partner(1), z_partner(-1)]
     for partner in near:
         tell(barrier, partner)
     loads[0].wait()
@@ -119,6 +122,8 @@
             pl.semaphore_wait(known_sem.at[r], 2)
 
     tell_known(0)
+    for i in range(1, n_x):
+        tell(known_sem.at[3], x_partner(i))
 
     pos = me * tok + lax.broadcasted_iota(jnp.int32, (8, tok), 1)
     first = jnp.zeros((8, tok), jnp.int32)
@@ -251,6 +256,8 @@
         squares = squares + jnp.sum((part * part).reshape(HD // 8, 8, tok), axis=0)
         dq_ref[:, h * HD : (h + 1) * HD] = part.T.astype(BF16)
     hear_known(2)
+    if n_x > 1:
+        pl.semaphore_wait(known_sem.at[3], n_x - 1)
     for i in range(pieces):
         rows = slice(i * PIECE, (i + 1) * PIECE)
         g_copy(1, -1, i).wait_recv()
@@ -260,10 +267,15 @@
         out, begin = (dk_ref, i * PIECE) if i * PIECE < tok else (dv_ref, i * PIECE - tok)
         out[begin : begin + PIECE, :] = part.astype(BF16)
 
+    def away(i, n):
+        return min(i % n, n - i % n)
+
+    def plane_away(i):
+        return -away(i // n_head, n_x) - away(i % n_head // 2, max(n_head // 2, 1))
+
     levels = (
-        (head_partner, range(1, n_head), mh, sum_head),
-        (x_partner, range(1, n_x), my_x, sum_x),
-        (z_partner, sorted(range(1, n_z), key=lambda i: -min(i, n_z - i)), my_z, sum_z),
+        (plane_partner, sorted(range(1, n_x * n_head), key=plane_away), my_x * n_head + mh, sum_plane),
+        (z_partner, sorted(range(1, n_z), key=lambda i: -away(i, n_z)), my_z, sum_z),
     )
     for level, (partner, offsets, mine, slots) in enumerate(levels):
         n = slots.shape[0]
@@ -277,23 +289,22 @@
                 device_id=partner(i),
                 device_id_type=MESH,
             ).start()
-        if n > 1:
-            others = slots.at[pl.ds(0, n - 1)]
-            pltpu.make_async_copy(others, others, s_recv.at[level]).wait()
-        squares = slots[0]
-        for i in range(1, n):
-            squares = squares + slots[i]
+        if level == 1:
+            for d in range(1, 2 * HOP - 1):
+                for i in range(pieces):
+                    kv_copy(0, d, 1, i).wait_send()
+                    g_copy(d, -1, i).wait_send()
+        others = slots.at[pl.ds(0, n - 1)]
+        pltpu.make_async_copy(others, others, s_recv.at[level]).wait()
+        parts = [slots[i] for i in range(n)]
+        while len(parts) > 1:
+            parts = [sum(parts[i : i + 2][1:], parts[i]) for i in range(0, len(parts), 2)]
+        squares = parts[0]
     rms_ref[...] = jnp.broadcast_to(jnp.sqrt(jnp.sum(squares) / count_all), rms_ref.shape)
 
     for level, (_, _, _, slots) in enumerate(levels):
-        n = slots.shape[0]
-        if n > 1:
-            others = slots.at[pl.ds(0, n - 1)]
-            pltpu.make_async_copy(others, others, s_send.at[level]).wait()
-    for d in range(1, 2 * HOP - 1):
-        for i in range(pieces):
-            kv_copy(0, d, 1, i).wait_send()
-            g_copy(d, -1, i).wait_send()
+        others = slots.at[pl.ds(0, slots.shape[0] - 1)]
+        pltpu.make_async_copy(others, others, s_send.at[level]).wait()
 
 
 def local(mesh_sizes, queries, keys, values, out_grad, doc_lengths):
@@ -310,10 +321,10 @@
     dq, dk, dv, rms = pl.pallas_call(
         partial(kernel, (n_x, n_z, n_head, docs), HD ** (-0.5), float(count_all)),
         out_shape=(
-            jax.ShapeDtypeStruct((tok, q_cols), BF16),
-            jax.ShapeDtypeStruct((tok, HD), BF16),
-            jax.ShapeDtypeStruct((tok, HD), BF16),
-            jax.ShapeDtypeStruct((8, HD), F32),
+            pltpu.VMEM((tok, q_cols), BF16),
+            pltpu.VMEM((tok, HD), BF16),
+            pltpu.VMEM((tok, HD), BF16),
+            pltpu.VMEM((8, HD), F32),
         ),
         in_specs=[pl.BlockSpec(memory_space=pltpu.SMEM)] + [pl.BlockSpec(memory_space=pl.ANY)] * 4,
         out_specs=(vmem,) * 4,
@@ -337,17 +348,16 @@
             pltpu.VMEM((1, wide), F32),
             pltpu.VMEM((blocks, 2 * tok, HD), BF16),
             pltpu.VMEM((blocks, 2 * tok, HD), BF16),
-            pltpu.VMEM((n_head, 8, HD), F32),
-            pltpu.VMEM((n_x, 8, HD), F32),
+            pltpu.VMEM((n_x * n_head, 8, HD), F32),
             pltpu.VMEM((n_z, 8, HD), F32),
             pltpu.SemaphoreType.DMA((4,)),
             pltpu.SemaphoreType.DMA((blocks, pieces)),
             pltpu.SemaphoreType.DMA((blocks, pieces)),
             pltpu.SemaphoreType.DMA((blocks, pieces)),
             pltpu.SemaphoreType.DMA((blocks, pieces)),
-            pltpu.SemaphoreType.DMA((3,)),
-            pltpu.SemaphoreType.DMA((3,)),
-            pltpu.SemaphoreType.REGULAR((3,)),
+            pltpu.SemaphoreType.DMA((2,)),
+            pltpu.SemaphoreType.DMA((2,)),
+            pltpu.SemaphoreType.REGULAR((4,)),
         ],
         compiler_params=pltpu.CompilerParams(
             collective_id=0, has_side_effects=True, vmem_limit_bytes=56 * 1024 * 1024

time: 95.8 us -> 91.9 us (0.959)
  Pallas kernels: 90.5 us -> 88.6 us
  local copies, waits for them, and re-layouts: 4.35 us -> 2.49 us
    pallas_call x1, Pallas kernels: 90.5 us -> 88.6 us  [local(): pl.pallas_call(partial(kernel, (n_x, n_z, n_head, docs), HD ** (-0.5), fl...]
    unnamed x7 -> x3, local copies, waits for them, and re-layouts: 3.16 us -> 1.97 us
where the time goes in v3:
time: 91.9 us; the launch traced here: 91.7 us
  Pallas kernels  88.6 us (96%)
  local copies, waits for them, and re-layouts  2.49 us (3%)
    pallas_call x1, Pallas kernels, local(): pl.pallas_call(partial(kernel, (n_x, n_z, n_head, docs), HD ** (-0.5), fl...  88.6 us
    unnamed x3, local copies, waits for them, and re-layouts  1.97 us

profile of v3, /device:TPU:1, one launch (start us, length us, event | category | flops | bytes accessed | tf_op | source)
XLA Modules:
  0.0 91.7 jit_solution(9378379639447394319)
XLA Ops:
  0.6 88.6 %shard_map.84 = (bf16[128,1536]{1,0:T(8,128)(2,1)S(1)}, bf16[128,128]{1,0:T(8,128)(2,1)S(1)}, bf16[128,128]{1,0:T(8,128)(2,1)S(1)}, f32[8,128]{1,0:T(8,128)S(1)}) custom-call(s32[32]{0:T(128)} %doc_ref.1, bf16[128,1536]{1,0:T(8,128)(2,1)} %q_hbm.1, bf16[128,128]{1,0:T(8,128)(2,1)} %k_hbm.1, bf16[128,128]{1,0:T(8,128)(2,1)} %v_hbm.1, bf16[128,1536]{1,0:T(8,128)(2,1)} %do_hbm.1), custom_call_target="tpu_custom_call" | custom-call | flops 2264924160 | bytes 1179648 | tf_op jit(solution)/shard_map/pallas_call | solution.py:321
  89.2 0.5 slice.3
  89.7 0.7 copy.12
  90.5 0.6 copy.13
  91.1 0.6 copy.14

commit v4 on v3

--- a/solution.py
+++ b/solution.py
@@ -279,7 +279,7 @@
     )
     for level, (partner, offsets, mine, slots) in enumerate(levels):
         n = slots.shape[0]
-        slots[mine] = squares
+        slots[mine] = jnp.sum(squares, axis=0, keepdims=True)
         for i in offsets:
             pltpu.make_async_remote_copy(
                 src_ref=slots.at[mine],
@@ -348,8 +348,8 @@
             pltpu.VMEM((1, wide), F32),
             pltpu.VMEM((blocks, 2 * tok, HD), BF16),
             pltpu.VMEM((blocks, 2 * tok, HD), BF16),
-            pltpu.VMEM((n_x * n_head, 8, HD), F32),
-            pltpu.VMEM((n_z, 8, HD), F32),
+            pltpu.VMEM((n_x * n_head, 1, HD), F32),
+            pltpu.VMEM((n_z, 1, HD), F32),
             pltpu.SemaphoreType.DMA((4,)),
             pltpu.SemaphoreType.DMA((blocks, pieces)),
             pltpu.SemaphoreType.DMA((blocks, pieces)),

time: 91.9 us -> 86.6 us (0.942)
  Pallas kernels: 88.6 us -> 83.3 us
    pallas_call x1, Pallas kernels: 88.6 us -> 83.3 us  [local(): pl.pallas_call(partial(kernel, (n_x, n_z, n_head, docs), HD ** (-0.5), fl...]
where the time goes in v4:
time: 86.6 us; the launch traced here: 86.4 us
  Pallas kernels  83.3 us (96%)
  local copies, waits for them, and re-layouts  2.49 us (3%)
    pallas_call x1, Pallas kernels, local(): pl.pallas_call(partial(kernel, (n_x, n_z, n_head, docs), HD ** (-0.5), fl...  83.3 us
    unnamed x3, local copies, waits for them, and re-layouts  1.97 us

profile of v4, /device:TPU:1, one launch (start us, length us, event | category | flops | bytes accessed | tf_op | source)
XLA Modules:
  0.0 86.4 jit_solution(17039840507569715353)
XLA Ops:
  0.6 83.3 %shard_map.84 = (bf16[128,1536]{1,0:T(8,128)(2,1)S(1)}, bf16[128,128]{1,0:T(8,128)(2,1)S(1)}, bf16[128,128]{1,0:T(8,128)(2,1)S(1)}, f32[8,128]{1,0:T(8,128)S(1)}) custom-call(s32[32]{0:T(128)} %doc_ref.1, bf16[128,1536]{1,0:T(8,128)(2,1)} %q_hbm.1, bf16[128,128]{1,0:T(8,128)(2,1)} %k_hbm.1, bf16[128,128]{1,0:T(8,128)(2,1)} %v_hbm.1, bf16[128,1536]{1,0:T(8,128)(2,1)} %do_hbm.1), custom_call_target="tpu_custom_call" | custom-call | flops 2264924160 | bytes 1179648 | tf_op jit(solution)/shard_map/pallas_call | solution.py:321
  84.0 0.5 slice.3
  84.5 0.7 copy.12
  85.2 0.6 copy.13
  85.8 0.6 copy.14
